TPU v7x, 512 devices: a whole 4x4x16 slice. The times are simulated.
512 devices in a mesh: ctx: 128 (over y, z_lo, x), tp: 4 (over z_hi, core).
Axes of the slice: x: 4, y: 4, z: 16 (z_hi: 2, z_lo: 8; z = z_hi * 8 + z_lo), core: 2. Of those that a mesh axis runs over, the one named last changes fastest.
Arguments:
- query_proj: bfloat16 [16384, 4096], P('ctx', 'tp'), may hold values from -6 to 6
- key_proj: bfloat16 [16384, 4096], P('ctx', 'tp'), may hold values from -6 to 6
- value_proj: bfloat16 [16384, 4096], P('ctx', 'tp'), may hold values from -6 to 6
- cotangent: bfloat16 [16384, 4096], P('ctx', 'tp'), may hold values from -6 to 6
- filter_taps: float32 [16384, 4096], P('ctx', 'tp'), may hold values from -1 to 1
- short_weights: float32 [3, 3, 4096], P(None, None, 'tp'), may hold values from -3.5 to 3.5
Outputs:
- gated_out: bfloat16 [16384, 4096], P('ctx', 'tp')
- query_grad: bfloat16 [16384, 4096], P('ctx', 'tp')
- key_grad: bfloat16 [16384, 4096], P('ctx', 'tp')
- value_grad: bfloat16 [16384, 4096], P('ctx', 'tp')
- filter_grad: float32 [16384, 4096], P('ctx', 'tp')
- short_grad: float32 [3, 3, 4096], P(None, None, 'tp')
All inputs are finite; a program needn't handle non-finite values.
Results may differ from a plain program's by a relative error of at most 0.0065.
Values may be sent and summed in bfloat16 or wider, within the bound.
A program may use at most 64 MiB of HBM per device.

v0:
```python
import math
import jax
import jax.numpy as jnp
from jax import lax
from jax.sharding import PartitionSpec as P


def from_behind(array, axis, by):
    peers = lax.axis_size(axis)
    pairs = [(i, i + by) for i in range(peers) if 0 <= i + by < peers]
    return lax.ppermute(array, axis, pairs)


def contract(form, left, right):
    return jnp.einsum(
        form, left, right, precision=lax.Precision.HIGHEST, preferred_element_type=jnp.float32
    )


def dft_tables(rows, cols, period):
    row_ids = lax.broadcasted_iota(jnp.int32, (rows, cols), 0)
    col_ids = lax.broadcasted_iota(jnp.int32, (rows, cols), 1)
    angle = 2.0 * math.pi / period * (row_ids * col_ids % period).astype(jnp.float32)
    return (jnp.cos(angle), jnp.sin(angle))


def make_plan(seq_len):
    small_len = int(math.isqrt(2 * seq_len))
    while seq_len % small_len:
        small_len -= 1
    large_len = 2 * seq_len // small_len
    large_cos, large_sin = dft_tables(large_len // 2, large_len, large_len)
    small_cos, small_sin = dft_tables(small_len, small_len, small_len)
    twist_cos, twist_sin = dft_tables(large_len, small_len, small_len * large_len)
    fwd_large = jnp.stack([large_cos, -large_sin], axis=1)
    fwd_small = jnp.stack([jnp.stack([small_cos, -small_sin]), jnp.stack([small_sin, small_cos])])
    inv_small = jnp.stack([jnp.stack([small_cos, small_sin]), jnp.stack([-small_sin, small_cos])])
    inv_large = jnp.stack([large_cos, -large_sin])
    return (small_len, large_len, fwd_large, fwd_small, inv_small, inv_large, twist_cos, twist_sin)


def forward_spec(signal, dft_plan):
    small_len, large_len, fwd_large, fwd_small, inv_small, inv_large, twist_cos, twist_sin = (
        dft_plan
    )
    cube = signal.reshape(signal.shape[0], large_len // 2, small_len)
    section_one = contract("cba,bpk->cpka", cube, fwd_large)
    real_one = section_one[:, 0]
    imag_one = section_one[:, 1]
    section_two = jnp.stack(
        [real_one * twist_cos + imag_one * twist_sin, imag_one * twist_cos - real_one * twist_sin],
        axis=1,
    )
    return contract("cpka,pqaj->cqkj", section_two, fwd_small)


def inverse_half(spec, dft_plan):
    small_len, large_len, fwd_large, fwd_small, inv_small, inv_large, twist_cos, twist_sin = (
        dft_plan
    )
    section_one = contract("cqkj,qpja->cpka", spec, inv_small)
    real_one = section_one[:, 0]
    imag_one = section_one[:, 1]
    section_two = jnp.stack(
        [real_one * twist_cos - imag_one * twist_sin, imag_one * twist_cos + real_one * twist_sin],
        axis=1,
    )
    signal = contract("cpka,pbk->cba", section_two, inv_large)
    return signal.reshape(signal.shape[0], -1) / float(small_len * large_len)


def complex_mul(left, right):
    left_real, left_imag = (left[:, 0], left[:, 1])
    right_real, right_imag = (right[:, 0], right[:, 1])
    return jnp.stack(
        [
            left_real * right_real - left_imag * right_imag,
            left_real * right_imag + left_imag * right_real,
        ],
        axis=1,
    )


def conj_mul(left, right):
    left_real, left_imag = (left[:, 0], left[:, 1])
    right_real, right_imag = (right[:, 0], right[:, 1])
    return jnp.stack(
        [
            left_real * right_real + left_imag * right_imag,
            left_real * right_imag - left_imag * right_real,
        ],
        axis=1,
    )


def conv_forward(prod_chan, filter_spec, dft_plan):
    prod_spec = forward_spec(prod_chan.astype(jnp.float32), dft_plan)
    conv_chan = inverse_half(complex_mul(prod_spec, filter_spec), dft_plan).astype(jnp.bfloat16)
    return (conv_chan, prod_spec)


def conv_backward(grad_chan, filter_spec, prod_spec, dft_plan, grad_scale):
    grad_spec = forward_spec(grad_chan.astype(jnp.float32), dft_plan)
    dconv_chan = inverse_half(conj_mul(filter_spec, grad_spec), dft_plan).astype(jnp.bfloat16)
    dfilter_chan = inverse_half(conj_mul(prod_spec, grad_spec), dft_plan) * grad_scale
    return (dconv_chan, dfilter_chan)


def receive_filter(filter_taps, dft_plan):
    filter_chan = lax.all_to_all(filter_taps.T, "ctx", split_axis=0, concat_axis=1, tiled=True)
    return forward_spec(filter_chan, dft_plan)


def return_filter(dfilter_chan):
    return (
        lax.all_to_all(
            dfilter_chan.astype(jnp.bfloat16), "ctx", split_axis=1, concat_axis=0, tiled=True
        )
        .astype(dfilter_chan.dtype)
        .T
    )


def causal_taps(extended, weights, length, axis):
    rim_rows = len(weights) - 1
    summed = weights[0] * lax.slice_in_dim(extended, rim_rows, rim_rows + length, axis=axis)
    for offset in range(1, len(weights)):
        summed = summed + weights[offset] * lax.slice_in_dim(
            extended, rim_rows - offset, rim_rows - offset + length, axis=axis
        )
    return summed


def reverse_taps(extended, weights, length, axis):
    summed = weights[0] * lax.slice_in_dim(extended, 0, length, axis=axis)
    for offset in range(1, len(weights)):
        summed = summed + weights[offset] * lax.slice_in_dim(
            extended, offset, offset + length, axis=axis
        )
    return summed


def tap_grads(grad_in, extended, tap_count, length, axis):
    rim_rows = tap_count - 1
    rows = [
        jnp.sum(
            grad_in
            * lax.slice_in_dim(extended, rim_rows - offset, rim_rows - offset + length, axis=axis),
            axis=axis,
        )
        for offset in range(tap_count)
    ]
    return jnp.stack(rows, axis=1)


def shards(query_proj, key_proj, value_proj, cotangent, filter_taps, short_weights):
    tokens = query_proj.shape[0]
    tap_count = short_weights.shape[1]
    rim_rows = tap_count - 1
    seq_len = tokens * lax.axis_size("ctx")
    grad_scale = 1.0 / math.sqrt(seq_len)
    dft_plan = make_plan(seq_len)
    stacked = jnp.stack([query_proj, key_proj, value_proj])
    prev_rim = from_behind(stacked[:, tokens - rim_rows :], "ctx", 1)
    extended = jnp.concatenate([prev_rim, stacked], axis=1).astype(jnp.float32)
    weights = [short_weights[:, offset, None, :] for offset in range(tap_count)]
    short_out = causal_taps(extended, weights, tokens, 1)
    product = (short_out[1] * short_out[2]).astype(jnp.bfloat16)
    cot_wide = cotangent.astype(jnp.float32)
    gate_grad = (cot_wide * short_out[0]).astype(jnp.bfloat16)
    filter_spec = receive_filter(filter_taps, dft_plan)
    prod_chan = lax.all_to_all(product.T, "ctx", split_axis=0, concat_axis=1, tiled=True)
    conv_chan, prod_spec = conv_forward(prod_chan, filter_spec, dft_plan)
    conv_tok = lax.all_to_all(conv_chan, "ctx", split_axis=1, concat_axis=0, tiled=True)
    grad_chan = lax.all_to_all(gate_grad.T, "ctx", split_axis=0, concat_axis=1, tiled=True)
    dconv_chan, dfilter_chan = conv_backward(
        grad_chan, filter_spec, prod_spec, dft_plan, grad_scale
    )
    dconv_tok = lax.all_to_all(dconv_chan, "ctx", split_axis=1, concat_axis=0, tiled=True)
    filter_grad = return_filter(dfilter_chan)
    conv_wide = conv_tok.T.astype(jnp.float32)
    dconv_wide = dconv_tok.T.astype(jnp.float32)
    gated = (short_out[0] * conv_wide).astype(jnp.bfloat16)
    token_grads = jnp.stack(
        [cot_wide * conv_wide, dconv_wide * short_out[2], dconv_wide * short_out[1]]
    )
    next_rim = from_behind(token_grads[:, :rim_rows], "ctx", -1)
    grad_ext = jnp.concatenate([token_grads, next_rim], axis=1)
    inputs_grad = reverse_taps(grad_ext, weights, tokens, 1).astype(jnp.bfloat16)
    weight_part = tap_grads(token_grads, extended, tap_count, tokens, 1)
    short_grad = lax.psum(weight_part, "ctx") * grad_scale
    results = (gated, inputs_grad[0], inputs_grad[1], inputs_grad[2])
    return (results[0], results[1], results[2], results[3], filter_grad, short_grad)


def solution(mesh):
    placed = (
        P("ctx", "tp"),
        P("ctx", "tp"),
        P("ctx", "tp"),
        P("ctx", "tp"),
        P("ctx", "tp"),
        P(None, None, "tp"),
    )
    return jax.shard_map(
        shards,
        mesh=mesh,
        in_specs=placed,
        out_specs=(
            P("ctx", "tp"),
            P("ctx", "tp"),
            P("ctx", "tp"),
            P("ctx", "tp"),
            P("ctx", "tp"),
            P(None, None, "tp"),
        ),
        check_vma=False,
    )
```

profile of v0, /device:TPU:256, one launch (start us, length us, event | category | flops | bytes accessed | tf_op | source)
XLA Modules:
  0.0 1284.4 jit_solution(9625832330967187007)
XLA Ops:
  4.9 3.4 collective-permute-start
  10.9 2.0 maximum_convert_fusion
  12.9 2.4 multiply_add_fusion
  17.2 17.1 %all-to-all-start.3 = ((bf16[128,8,128]{2,1,0:T(8,128)(2,1)}), bf16[128,8,128]{2,1,0:T(8,128)(2,1)S(1)}, u32[]{:S(2)}, u32[]{:S(2)}) async-start(bf16[128,8,128]{2,1,0:T(8,128)(2,1)} %fusion.92), calls=%async_computation.3 | async-start | bytes 524288 | tf_op jit(solution)/shard_map/all_to_all | solution.py:175
  34.3 2.0 copy.69
  36.4 18.0 %all-to-all-done.3 = bf16[128,8,128]{2,1,0:T(8,128)(2,1)S(1)} async-done(((bf16[128,8,128]{2,1,0:T(8,128)(2,1)}), bf16[128,8,128]{2,1,0:T(8,128)(2,1)S(1)}, u32[]{:S(2)}, u32[]{:S(2)}) %all-to-all-start.3) | async-done | bytes 262176 | tf_op jit(solution)/shard_map/all_to_all | solution.py:175
  54.4 8.1 all-to-all-start.1
  66.2 3.3 convolution_bitcast_fusion.1
  69.5 23.2 %all-to-all-done.1 = f32[128,8,128]{2,1,0:T(8,128)} async-done(((f32[128,8,128]{2,1,0:T(8,128)}), f32[128,8,128]{2,1,0:T(8,128)}, u32[]{:S(2)}, u32[]{:S(2)}) %all-to-all-start.1) | async-done | bytes 524320 | tf_op jit(solution)/shard_map/all_to_all | solution.py:110
  92.7 3.1 convolution_bitcast_fusion
  96.8 2.0 fusion.36
  98.8 2.0 fusion.30
  101.7 3.9 fusion.39
  108.0 28.0 %all_to_all.78 = bf16[8,128,128]{2,0,1:T(8,128)(2,1)S(1)} all-to-all(bf16[8,128,128]{2,0,1:T(8,128)(2,1)S(1)} %copy.84), channel_id=1, replica_groups=mesh['ctx'=128,'tp'=4] {'ctx'}, dimensions={1} | all-to-all | bytes 524288 | tf_op jit(solution)/shard_map/all_to_all | solution.py:179
  137.1 27.6 %all_to_all.79 = bf16[128,8,128]{2,1,0:T(8,128)(2,1)S(1)} all-to-all(bf16[128,8,128]{2,1,0:T(8,128)(2,1)S(1)} %get-tuple-element.44), channel_id=1, replica_groups=mesh['ctx'=128,'tp'=4] {'ctx'}, dimensions={0} | all-to-all | bytes 524288 | tf_op jit(solution)/shard_map/all_to_all | solution.py:172
  165.9 2.0 fusion.27
  168.7 3.6 fusion.42
  172.3 3.6 fusion.33
  175.9 2.0 multiply_subtract_fusion
  180.3 8.1 all-to-all-start.2
  188.3 2.9 fusion.81
  192.1 16.2 %all-to-all-done.2 = bf16[8,128,128]{2,0,1:T(8,128)(2,1)} async-done(((bf16[8,128,128]{2,0,1:T(8,128)(2,1)}), bf16[8,128,128]{2,0,1:T(8,128)(2,1)}, u32[]{:S(2)}, u32[]{:S(2)}) %all-to-all-start.2) | async-done | bytes 262176 | tf_op jit(solution)/shard_map/all_to_all | solution.py:174
  208.3 7.9 all-to-all-start.5
  216.3 2.0 fusion.84
  219.6 1.9 copy.85
  222.7 13.5 %all-to-all-done.5 = bf16[8,128,128]{2,0,1:T(8,128)(2,1)} async-done(((bf16[8,128,128]{2,0,1:T(8,128)(2,1)}), bf16[8,128,128]{2,0,1:T(8,128)(2,1)}, u32[]{:S(2)}, u32[]{:S(2)}) %all-to-all-start.5) | async-done | bytes 262176 | tf_op jit(solution)/shard_map/all_to_all | solution.py:116
  236.2 1.8 convert_bitcast_fusion
  238.8 2.0 copy.96
  240.9 1.7 copy.86
  242.6 2.2 pad_maximum_fusion
  244.9 5.2 multiply_reduce_fusion.2
  250.1 1029.7 %psum.7 = f32[3,3,1024]{2,0,1:T(4,128)S(1)} all-reduce(f32[3,3,1024]{2,0,1:T(4,128)S(1)} %pad_maximum_fusion.15), channel_id=1, replica_groups=mesh['ctx'=128,'tp'=4] {'ctx'}, use_global_device_ids=true, to_apply=%region_3.4 | all-reduce | flops 9216 | bytes 73728 | tf_op jit(solution)/shard_map/psum | solution.py:191
  (103 shorter events, 30.9 us)
Async XLA Ops:
  0.6 7.7 copy-start.30
  0.6 7.7 copy-start.22
  1.8 7.9 copy-start.11
  3.1 6.6 copy-start.12
  4.3 5.4 copy-start.13
  4.9 4.8 collective-permute-start
  8.3 4.5 copy-start.23
  8.4 4.5 copy-start.25
  8.6 6.7 copy-start.9
  15.3 1.2 copy-start
  17.2 37.2 %all-to-all-start.3 = ((bf16[128,8,128]{2,1,0:T(8,128)(2,1)}), bf16[128,8,128]{2,1,0:T(8,128)(2,1)S(1)}, u32[]{:S(2)}, u32[]{:S(2)}) async-start(bf16[128,8,128]{2,1,0:T(8,128)(2,1)} %fusion.92), calls=%async_computation.3 | async-start | bytes 524288 | tf_op jit(solution)/shard_map/all_to_all | solution.py:175
  54.4 8.4 copy-start.20
  54.4 38.3 %all-to-all-start.1 = ((f32[128,8,128]{2,1,0:T(8,128)}), f32[128,8,128]{2,1,0:T(8,128)}, u32[]{:S(2)}, u32[]{:S(2)}) async-start(f32[128,8,128]{2,1,0:T(8,128)} %bitcast.253), calls=%async_computation.1 | async-start | bytes 1048576 | tf_op jit(solution)/shard_map/all_to_all | solution.py:110
  92.7 3.1 copy-start.8
  95.8 1.0 copy-start.19
  100.7 1.0 copy-start.17
  105.9 30.1 %copy-start.1 = (f32[3,128,1024]{1,2,0:T(8,128)S(1)}, f32[3,128,1024]{1,2,0:T(8,128)}, u32[]{:S(2)}) copy-start(f32[3,128,1024]{1,2,0:T(8,128)} %copy-done) | copy-start | bytes 4718596
  107.8 56.8 %copy-start.15 = (f32[128,1,256]{0,2,1:T(8,128)S(1)}, f32[128,1,256]{0,2,1:T(8,128)}, u32[]{:S(2)}) copy-start(f32[128,1,256]{0,2,1:T(8,128)} %copy-done.14) | copy-start | bytes 393220
  177.9 10.4 copy-start.28
  180.3 36.0 %copy-start.10 = (bf16[128,1024]{0,1:T(8,128)(2,1)S(1)}, bf16[128,1024]{0,1:T(8,128)(2,1)}, u32[]{:S(2)}) copy-start(bf16[128,1024]{0,1:T(8,128)(2,1)} %copy-done.9) | copy-start | bytes 786436
  180.3 28.0 %all-to-all-start.2 = ((bf16[8,128,128]{2,0,1:T(8,128)(2,1)}), bf16[8,128,128]{2,0,1:T(8,128)(2,1)}, u32[]{:S(2)}, u32[]{:S(2)}) async-start(bf16[8,128,128]{2,0,1:T(8,128)(2,1)} %copy.76), calls=%async_computation.2 | async-start | bytes 524288 | tf_op jit(solution)/shard_map/all_to_all | solution.py:174
  208.3 27.9 %all-to-all-start.5 = ((bf16[8,128,128]{2,0,1:T(8,128)(2,1)}), bf16[8,128,128]{2,0,1:T(8,128)(2,1)}, u32[]{:S(2)}, u32[]{:S(2)}) async-start(bf16[8,128,128]{2,0,1:T(8,128)(2,1)} %copy.91), calls=%async_computation.5 | async-start | bytes 524288 | tf_op jit(solution)/shard_map/all_to_all | solution.py:116
  216.2 2.0 copy-start.2
  216.2 2.0 copy-start.4
  218.3 1.3 copy-start.6
  218.3 19.7 %copy-start.21 = (bf16[128,1024]{0,1:T(8,128)(2,1)S(1)}, bf16[128,1024]{0,1:T(8,128)(2,1)}, u32[]{:S(2)}) copy-start(bf16[128,1024]{0,1:T(8,128)(2,1)} %get-tuple-element.51) | copy-start | bytes 786436
  221.4 19.4 %collective-permute-start.1 = (f32[3,2,1024]{2,1,0:T(2,128)S(1)}, f32[3,2,1024]{2,1,0:T(2,128)S(1)}, u32[]{:S(2)}, u32[]{:S(2)}) collective-permute-start(f32[3,2,1024]{2,1,0:T(2,128)S(1)} %copy.85), channel_id=1, source_target_pairs={{4,0},{8,4},{12,8},{16,12},{20,16},{24,20},{28,24},{32,28},{36,32}... | collective-permute-start | bytes 73736 | tf_op jit(solution)/shard_map/ppermute | solution.py:11
  242.6 2.2 copy-start.3
  242.6 2.2 copy-start.5
  242.6 2.3 copy-start.7
  242.6 2.3 copy-start.24
  242.6 2.3 copy-start.26
  (5 other events, 4.5 us)
where the time goes:
time: 1290 us; the launch traced here: 1280 us
  blocking collectives  1090 us (84%)
  waiting for transfers between devices  72 us (6%)
  starting transfers between devices  45.9 us (4%)
  matrix products  29.9 us (2%)
  other arithmetic  26.8 us (2%)
  local copies, waits for them, and re-layouts  23.2 us (2%)
    psum x1, blocking collectives, shards(): short_grad = lax.psum(weight_part, 'ctx') * grad_scale  1030 us
    dot_general x12, matrix products, contract(): jnp.einsum(form, left, right, precision=lax.Precision.HIGHEST, preferred_...  29.9 us
    all_to_all x1, blocking collectives, shards(): lax.all_to_all(dconv_chan, 'ctx', split_axis=1, concat_axis=0, tiled=True)  28 us
    all_to_all x1, blocking collectives, shards(): lax.all_to_all(product.T, 'ctx', split_axis=0, concat_axis=1, tiled=True)  27.6 us
  transfers between devices with their start and end apart: 6, of which 5 were waited for; matrix products, arithmetic and copies ran while one was open for 2% of the time, Pallas kernels for 0%

commit v1 on v0

--- a/solution.py
+++ b/solution.py
@@ -188,7 +188,7 @@
     grad_ext = jnp.concatenate([token_grads, next_rim], axis=1)
     inputs_grad = reverse_taps(grad_ext, weights, tokens, 1).astype(jnp.bfloat16)
     weight_part = tap_grads(token_grads, extended, tap_count, tokens, 1)
-    short_grad = lax.psum(weight_part, "ctx") * grad_scale
+    short_grad = jnp.sum(lax.all_gather(weight_part, "ctx"), axis=0) * grad_scale
     results = (gated, inputs_grad[0], inputs_grad[1], inputs_grad[2])
     return (results[0], results[1], results[2], results[3], filter_grad, short_grad)
 

time: 1290 us -> 1220 us (0.946)
  the two profiles are of different devices: /device:TPU:256 before, /device:TPU:0 now
where the time goes in v1:
time: 1220 us
  waiting for transfers between devices  998 us (82%)
  blocking collectives  83.1 us (7%)
  starting transfers between devices  45.1 us (4%)
  matrix products  29.9 us (2%)
  other arithmetic  26.8 us (2%)
  local copies, waits for them, and re-layouts  20.3 us (2%)
  between operations  14.8 us (1%)
    all_gather x1, waiting for transfers between devices, shards(): lax.all_gather(weight_part, 'ctx')  932 us
    dot_general x12, matrix products, contract(): jnp.einsum(form, left, right, precision=lax.Precision.HIGHEST, preferred_...  29.9 us
    all_to_all x1, blocking collectives, shards(): lax.all_to_all(dconv_chan, 'ctx', split_axis=1, concat_axis=0, tiled=True)  28 us
    all_to_all x1, blocking collectives, shards(): lax.all_to_all(product.T, 'ctx', split_axis=0, concat_axis=1, tiled=True)  27.6 us
    all_to_all x1, blocking collectives, shards(): lax.all_to_all(conv_chan, 'ctx', split_axis=1, concat_axis=0, tiled=True)  27.6 us
  transfers between devices with their start and end apart: 6, of which 6 were waited for; matrix products, arithmetic and copies ran while one was open for 1% of the time, Pallas kernels for 0%

profile of v1, /device:TPU:0, one launch (start us, length us, event | category | flops | bytes accessed | tf_op | source)
XLA Modules:
  0.0 1218.4 jit_solution(12358425093221357213)
XLA Ops:
  15.3 2.0 maximum_convert_fusion
  17.3 2.4 multiply_add_fusion
  21.6 17.4 %all-to-all-start.3 = ((bf16[128,8,128]{2,1,0:T(8,128)(2,1)}), bf16[128,8,128]{2,1,0:T(8,128)(2,1)S(1)}, u32[]{:S(2)}, u32[]{:S(2)}) async-start(bf16[128,8,128]{2,1,0:T(8,128)(2,1)} %fusion.92), calls=%async_computation.3 | async-start | bytes 524288 | tf_op jit(solution)/shard_map/all_to_all | solution.py:175
  39.0 2.0 copy.68
  41.1 18.0 %all-to-all-done.3 = bf16[128,8,128]{2,1,0:T(8,128)(2,1)S(1)} async-done(((bf16[128,8,128]{2,1,0:T(8,128)(2,1)}), bf16[128,8,128]{2,1,0:T(8,128)(2,1)S(1)}, u32[]{:S(2)}, u32[]{:S(2)}) %all-to-all-start.3) | async-done | bytes 262176 | tf_op jit(solution)/shard_map/all_to_all | solution.py:175
  59.1 7.9 all-to-all-start.1
  71.0 3.3 convolution_bitcast_fusion.1
  74.3 23.2 %all-to-all-done.1 = f32[128,8,128]{2,1,0:T(8,128)} async-done(((f32[128,8,128]{2,1,0:T(8,128)}), f32[128,8,128]{2,1,0:T(8,128)}, u32[]{:S(2)}, u32[]{:S(2)}) %all-to-all-start.1) | async-done | bytes 524320 | tf_op jit(solution)/shard_map/all_to_all | solution.py:110
  97.4 3.1 convolution_bitcast_fusion
  101.5 1.9 fusion.36
  103.5 2.0 fusion.30
  106.4 3.8 fusion.39
  112.7 28.0 %all_to_all.78 = bf16[8,128,128]{2,0,1:T(8,128)(2,1)S(1)} all-to-all(bf16[8,128,128]{2,0,1:T(8,128)(2,1)S(1)} %copy.83), channel_id=1, replica_groups=mesh['ctx'=128,'tp'=4] {'ctx'}, dimensions={1} | all-to-all | bytes 524288 | tf_op jit(solution)/shard_map/all_to_all | solution.py:179
  140.8 27.6 %all_to_all.79 = bf16[128,8,128]{2,1,0:T(8,128)(2,1)S(1)} all-to-all(bf16[128,8,128]{2,1,0:T(8,128)(2,1)S(1)} %get-tuple-element.44), channel_id=1, replica_groups=mesh['ctx'=128,'tp'=4] {'ctx'}, dimensions={0} | all-to-all | bytes 524288 | tf_op jit(solution)/shard_map/all_to_all | solution.py:172
  169.6 2.0 fusion.27
  172.4 3.6 fusion.42
  176.0 3.6 fusion.33
  179.6 2.0 multiply_subtract_fusion
  181.6 1.4 fusion.75
  183.2 27.6 %all_to_all.80 = bf16[8,128,128]{2,0,1:T(8,128)(2,1)S(1)} all-to-all(bf16[8,128,128]{2,0,1:T(8,128)(2,1)S(1)} %copy.75), channel_id=1, replica_groups=mesh['ctx'=128,'tp'=4] {'ctx'}, dimensions={1} | all-to-all | bytes 524288 | tf_op jit(solution)/shard_map/all_to_all | solution.py:174
  210.9 1.3 pad_maximum_fusion.4
  212.2 1.9 copy.84
  214.1 1.3 collective-permute-start.1
  215.4 4.4 collective-permute-done.1
  219.8 1.7 copy.85
  221.5 2.2 pad_maximum_fusion
  223.8 5.2 multiply_reduce_fusion.2
  229.8 3.0 fusion.81
  233.6 17.0 %all-to-all-start.5 = ((bf16[8,128,128]{2,0,1:T(8,128)(2,1)}), bf16[8,128,128]{2,0,1:T(8,128)(2,1)S(1)}, u32[]{:S(2)}, u32[]{:S(2)}) async-start(bf16[8,128,128]{2,0,1:T(8,128)(2,1)} %copy.90), calls=%async_computation.5 | async-start | bytes 524288 | tf_op jit(solution)/shard_map/all_to_all | solution.py:116
  251.5 19.1 %all-to-all-done.5 = bf16[8,128,128]{2,0,1:T(8,128)(2,1)S(1)} async-done(((bf16[8,128,128]{2,0,1:T(8,128)(2,1)}), bf16[8,128,128]{2,0,1:T(8,128)(2,1)S(1)}, u32[]{:S(2)}, u32[]{:S(2)}) %all-to-all-start.5) | async-done | bytes 262176 | tf_op jit(solution)/shard_map/all_to_all | solution.py:116
  274.3 932.4 %all-gather.3.cloned.1.call-done = f32[384,3,1024]{2,1,0:T(4,128)} async-done(((f32[3,3,1024]{2,1,0:T(4,128)}), f32[384,3,1024]{2,1,0:T(4,128)}) %all-gather.3.cloned.1.call-update) | async-done | bytes 4718608 | tf_op jit(solution)/shard_map/all_gather | solution.py:191
  1206.7 4.0 reduce_sum.39
  (106 shorter events, 27.4 us)
Async XLA Ops:
  7.2 5.5 copy-start.29
  7.2 5.6 copy-start.22
  8.4 5.7 copy-start.12
  9.6 4.5 copy-start.13
  10.8 3.3 copy-start.14
  11.4 2.7 collective-permute-start
  12.8 4.5 copy-start.23
  12.8 4.5 copy-start.25
  13.0 6.7 copy-start.10
  19.7 1.2 copy-start
  21.6 37.4 %all-to-all-start.3 = ((bf16[128,8,128]{2,1,0:T(8,128)(2,1)}), bf16[128,8,128]{2,1,0:T(8,128)(2,1)S(1)}, u32[]{:S(2)}, u32[]{:S(2)}) async-start(bf16[128,8,128]{2,1,0:T(8,128)(2,1)} %fusion.92), calls=%async_computation.3 | async-start | bytes 524288 | tf_op jit(solution)/shard_map/all_to_all | solution.py:175
  59.1 8.4 copy-start.21
  59.1 38.3 %all-to-all-start.1 = ((f32[128,8,128]{2,1,0:T(8,128)}), f32[128,8,128]{2,1,0:T(8,128)}, u32[]{:S(2)}, u32[]{:S(2)}) async-start(f32[128,8,128]{2,1,0:T(8,128)} %bitcast.252), calls=%async_computation.1 | async-start | bytes 1048576 | tf_op jit(solution)/shard_map/all_to_all | solution.py:110
  67.0 1139.6 %all-gather.3.cloned.1.call-start = ((), (), s32[]{:S(2)}) async-start(), calls=%async_computation.6 | async-start | bytes 6340608 | tf_op jit(solution)/shard_map/all_gather | solution.py:191
  97.4 3.1 copy-start.8
  100.5 1.0 copy-start.20
  105.4 1.0 copy-start.18
  110.2 1.0 copy-start.28
  110.5 30.1 %copy-start.1 = (f32[3,128,1024]{1,2,0:T(8,128)S(1)}, f32[3,128,1024]{1,2,0:T(8,128)}, u32[]{:S(2)}) copy-start(f32[3,128,1024]{1,2,0:T(8,128)} %copy-done) | copy-start | bytes 4718596
  112.5 55.9 %copy-start.16 = (f32[128,1,256]{0,2,1:T(8,128)S(1)}, f32[128,1,256]{0,2,1:T(8,128)}, u32[]{:S(2)}) copy-start(f32[128,1,256]{0,2,1:T(8,128)} %copy-done.15) | copy-start | bytes 393220
  140.7 70.1 %copy-start.2 = (f32[1,128,1024]{1,2,0:T(8,128)}, f32[1,128,1024]{1,2,0:T(8,128)S(1)}, u32[]{:S(2)}) copy-start(f32[1,128,1024]{1,2,0:T(8,128)S(1)} %get-tuple-element.41) | copy-start | bytes 1572868
  140.8 70.1 %copy-start.4 = (f32[1,128,1024]{1,2,0:T(8,128)}, f32[1,128,1024]{1,2,0:T(8,128)S(1)}, u32[]{:S(2)}) copy-start(f32[1,128,1024]{1,2,0:T(8,128)S(1)} %get-tuple-element.42) | copy-start | bytes 1572868
  181.6 29.2 %copy-start.11 = (bf16[128,1024]{0,1:T(8,128)(2,1)S(1)}, bf16[128,1024]{0,1:T(8,128)(2,1)}, u32[]{:S(2)}) copy-start(bf16[128,1024]{0,1:T(8,128)(2,1)} %copy-done.10) | copy-start | bytes 786436
  210.9 1.3 copy-start.6
  214.1 5.7 collective-permute-start.1
  221.5 2.2 copy-start.3
  221.5 2.2 copy-start.5
  221.5 2.3 copy-start.7
  221.5 2.3 copy-start.24
  221.5 2.3 copy-start.26
  232.7 38.9 %copy-start.9 = (bf16[3,128,1024]{1,2,0:T(8,128)(2,1)S(1)}, bf16[3,128,1024]{1,2,0:T(8,128)(2,1)}, u32[]{:S(2)}) copy-start(bf16[3,128,1024]{1,2,0:T(8,128)(2,1)} %get-tuple-element.43) | copy-start | bytes 2359300
  233.6 37.0 %all-to-all-start.5 = ((bf16[8,128,128]{2,0,1:T(8,128)(2,1)}), bf16[8,128,128]{2,0,1:T(8,128)(2,1)S(1)}, u32[]{:S(2)}, u32[]{:S(2)}) async-start(bf16[8,128,128]{2,0,1:T(8,128)(2,1)} %copy.90), calls=%async_computation.5 | async-start | bytes 524288 | tf_op jit(solution)/shard_map/all_to_all | solution.py:116
  (4 other events, 3.6 us)
Sparse Core Ops, SparseCore 0:
  229.9 976.7 all-gather.2
